TPU v7x, 128 devices: a whole 4x4x4 slice. The times are simulated.
128 devices in a mesh: ctx: 16 (over z, y), chan: 8 (over x, core).
Axes of the slice: x: 4, y: 4, z: 4, core: 2. Of those that a mesh axis runs over, the one named last changes fastest.
Arguments:
- query_proj: bfloat16 [2048, 8192], P('ctx', 'chan'), may hold values from -6 to 6
- key_proj: bfloat16 [2048, 8192], P('ctx', 'chan'), may hold values from -6 to 6
- value_proj: bfloat16 [2048, 8192], P('ctx', 'chan'), may hold values from -6 to 6
- filters: bfloat16 [8192, 128], P('chan'), may hold values from -0.5 to 0.5
- out_weight: bfloat16 [8192, 8192], P('chan'), may hold values from -0.0625 to 0.0625
- cotangent: bfloat16 [2048, 8192], P('ctx', 'chan'), may hold values from -6 to 6
Outputs:
- mixed: bfloat16 [2048, 8192], P('ctx', 'chan')
- grad_query: bfloat16 [2048, 8192], P('ctx', 'chan')
- grad_key: bfloat16 [2048, 8192], P('ctx', 'chan')
- grad_value: bfloat16 [2048, 8192], P('ctx', 'chan')
- grad_filters: float32 [8192, 128], P('chan')
- grad_weight: bfloat16 [8192, 8192], P('chan', 'ctx')
All inputs are finite; a program needn't handle non-finite values.
Results may differ from a plain program's by a relative error of at most 0.019.
Values may be sent and summed in bfloat16 or wider, within the bound.
A program may use at most 128 MiB of HBM per device.

v0:
```python
import jax
import jax.numpy as jnp
from jax import lax
from jax.sharding import PartitionSpec as P


def passed_along(block, axis, distance):
    devices = range(lax.axis_size(axis))
    route = [(i - distance, i) for i in devices if i - distance in devices]
    return lax.ppermute(block, axis, route)


def tap_sweep(source, taps_t, length, start_base, sign):
    group_size = 8
    tap_count = taps_t.shape[0]

    def one_group(group, running):
        for inner in range(group_size):
            offset = group * group_size + inner
            start = (start_base + sign * offset).astype(jnp.int32)
            rows = lax.dynamic_slice_in_dim(source, start, length, 0)
            running = running + rows * lax.dynamic_index_in_dim(taps_t, offset, 0, False)
        return running

    initial = jnp.zeros((length, source.shape[1]), jnp.float32)
    return lax.fori_loop(0, tap_count // group_size, one_group, initial)


def per_device(query_proj, key_proj, value_proj, filters, out_weight, cotangent):
    length, channels = query_proj.shape
    tap_count = filters.shape[1]
    taps_t = filters.astype(jnp.float32).T
    product = (key_proj.astype(jnp.float32) * value_proj.astype(jnp.float32)).astype(jnp.bfloat16)
    earlier = passed_along(product, "ctx", 1)
    ext_rows = jnp.concatenate([earlier, product], axis=0)
    ext_float = ext_rows.astype(jnp.float32)
    filtered = tap_sweep(ext_float, taps_t, length, tap_count, -1)
    gated_rows = (query_proj.astype(jnp.float32) * filtered).astype(jnp.bfloat16)
    partial_value = jnp.dot(gated_rows, out_weight, preferred_element_type=jnp.float32)
    mixed = lax.psum_scatter(
        partial_value.astype(jnp.bfloat16), "chan", scatter_dimension=1, tiled=True
    )
    full_cot = lax.all_gather(cotangent, "chan", axis=1, tiled=True)
    grad_gated = lax.dot_general(
        full_cot, out_weight, (((1,), (1,)), ((), ())), preferred_element_type=jnp.float32
    )
    grad_query = (grad_gated * filtered).astype(jnp.bfloat16)
    grad_filtered = (grad_gated * query_proj.astype(jnp.float32)).astype(jnp.bfloat16)
    grad_float = grad_filtered.astype(jnp.float32)
    following = passed_along(grad_filtered, "ctx", -1)
    grad_ext = jnp.concatenate([grad_float, following.astype(jnp.float32)], axis=0)
    grad_product = tap_sweep(grad_ext, taps_t, length, 0, 1)
    grad_key = (grad_product * value_proj.astype(jnp.float32)).astype(jnp.bfloat16)
    grad_value = (grad_product * key_proj.astype(jnp.float32)).astype(jnp.bfloat16)
    group_size = 8

    def tap_group(group, running):
        rows = []
        for inner in range(group_size):
            start = (tap_count - group * group_size - inner).astype(jnp.int32)
            source = lax.dynamic_slice_in_dim(ext_float, start, length, 0)
            rows.append(jnp.sum(grad_float * source, axis=0))
        stacked = jnp.stack(rows, axis=0)
        return lax.dynamic_update_slice_in_dim(
            running, stacked, (group * group_size).astype(jnp.int32), 0
        )

    tap_rows = lax.fori_loop(
        0, tap_count // group_size, tap_group, jnp.zeros((tap_count, channels), jnp.float32)
    )
    local_grad = tap_rows.T
    grad_filters = lax.psum(local_grad.astype(jnp.bfloat16), "ctx").astype(jnp.float32)
    partial_weight = lax.dot_general(
        gated_rows, full_cot, (((0,), (0,)), ((), ())), preferred_element_type=jnp.float32
    )
    grad_weight = lax.psum_scatter(
        partial_weight.astype(jnp.bfloat16), "ctx", scatter_dimension=1, tiled=True
    )
    return (mixed, grad_query, grad_key, grad_value, grad_filters, grad_weight)


def solution(mesh):
    placed = (
        P("ctx", "chan"),
        P("ctx", "chan"),
        P("ctx", "chan"),
        P("chan", None),
        P("chan", None),
        P("ctx", "chan"),
    )
    return jax.shard_map(
        per_device,
        mesh=mesh,
        in_specs=placed,
        out_specs=(
            P("ctx", "chan"),
            P("ctx", "chan"),
            P("ctx", "chan"),
            P("ctx", "chan"),
            P("chan", None),
            P("chan", "ctx"),
        ),
        check_vma=False,
    )
```

profile of v0, /device:TPU:1, one launch (start us, length us, event | category | flops | bytes accessed | tf_op | source)
XLA Modules:
  0.0 343.3 jit_solution(8738239071003889766)
XLA Ops:
  7.2 0.7 all-gather.2.cloned.1.call-update
  8.0 30.5 %all-gather.2.cloned.1.call-done = bf16[128,8192]{1,0:T(8,128)(2,1)} async-done(((bf16[128,1024]{1,0:T(8,128)(2,1)}), bf16[128,8192]{1,0:T(8,128)(2,1)}) %all-gather.2.cloned.1.call-update) | async-done | bytes 2097168 | tf_op jit(solution)/shard_map/all_gather | solution.py:43
  38.5 12.0 %fusion.21 = (f32[128,1024]{1,0:T(8,128)S(1)}, bf16[128,1024]{1,0:T(8,128)(2,1)S(1)}, f32[128,1024]{1,0:T(8,128)S(1)}) fusion(bf16[128,1024]{1,0:T(8,128)(2,1)} %param.12, bf16[128,8192]{1,0:T(8,128)(2,1)} %all-gather.2.cloned.1.call-done, bf16[1024,8192]{1,0:T(8,128)(2,1)} %param.16), kind=kOutput, calls=%fused_computation.58 | convolution fusion | flops 2148007936 | bytes 20447232 | tf_op jit(solution)/shard_map/dot_general | solution.py:44
  50.5 1.3 collective-permute-start.1
  52.0 8.0 %collective-permute-done.1 = bf16[128,1024]{1,0:T(8,128)(2,1)S(1)} collective-permute-done((bf16[128,1024]{1,0:T(8,128)(2,1)S(1)}, bf16[128,1024]{1,0:T(8,128)(2,1)S(1)}, u32[]{:S(2)}, u32[]{:S(2)}) %collective-permute-start.1) | collective-permute-done | bytes 262176 | tf_op jit(solution)/shard_map/ppermute | solution.py:10
  60.2 12.9 %while.52 = (s32[]{:T(128)}, f32[128,1024]{1,0:T(8,128)S(1)}, f32[256,1024]{1,0:T(8,128)S(1)}, f32[128,1024]{1,0:T(8,128)S(1)}, s32[]{:T(128)}, /*index=5*/s32[]...) while((s32[]{:T(128)}, f32[128,1024]{1,0:T(8,128)S(1)}, ...), condition=%wide.region_4.5_spmd.clone, body=%wide.region_3.4_spmd.clone.sunk | while | flops 2228275 | bytes 5342087 | solution.py:26
  60.3 0.7 fusion.30
  61.1 0.7 fusion.30
  61.9 0.7 fusion.30
  62.7 0.7 fusion.30
  63.5 0.7 fusion.30
  64.3 0.7 fusion.30
  65.2 0.7 fusion.30
  66.0 0.7 fusion.30
  66.8 0.7 fusion.30
  67.6 0.7 fusion.30
  68.4 0.7 fusion.30
  72.4 0.7 fusion.30
  73.1 2.0 fusion.16
  75.1 3.8 %collective-permute-start = (bf16[128,1024]{1,0:T(8,128)(2,1)S(1)}, bf16[128,1024]{1,0:T(8,128)(2,1)}, u32[]{:S(2)}, u32[]{:S(2)}) collective-permute-start(bf16[128,1024]{1,0:T(8,128)(2,1)S(1)} %get-tuple-element.522), channel_id=1, source_target_pairs={{0,8},{8,16},{16,24},{24,32},{32,40},{40,48},{48,56},{56,64},{64,7... | collective-permute-start | bytes 786440 | tf_op jit(solution)/shard_map/ppermute | solution.py:10
  78.9 3.8 %collective-permute-done = bf16[128,1024]{1,0:T(8,128)(2,1)} collective-permute-done((bf16[128,1024]{1,0:T(8,128)(2,1)S(1)}, bf16[128,1024]{1,0:T(8,128)(2,1)}, u32[]{:S(2)}, u32[]{:S(2)}) %collective-permute-start) | collective-permute-done | bytes 262176 | tf_op jit(solution)/shard_map/ppermute | solution.py:10
  82.7 1.1 maximum_convert_fusion
  83.8 13.4 %while.50 = (s32[]{:T(128)}, bf16[128,1024]{1,0:T(8,128)(2,1)S(1)}, f32[256,1024]{1,0:T(8,128)S(1)}, f32[128,1024]{1,0:T(8,128)S(1)}, s32[]{:T(128)}, /*index=5*...) while((s32[]{:T(128)}, bf16[128,1024]{1,0:T(8,128)(2,1)S(1)}, ...), condition=%wide.region_14.15_spmd, body=%wide.region_5.14_spmd.sunk | while | flops 2088998 | bytes 4833935 | solution.py:68
  83.9 0.7 multiply_reduce_fusion.9
  84.7 0.7 multiply_reduce_fusion.9
  85.5 0.7 multiply_reduce_fusion.9
  86.4 0.7 multiply_reduce_fusion.9
  87.2 0.7 multiply_reduce_fusion.9
  88.1 0.7 multiply_reduce_fusion.9
  88.9 0.7 multiply_reduce_fusion.9
  89.7 0.7 multiply_reduce_fusion.9
  90.6 0.7 multiply_reduce_fusion.9
  91.4 0.7 multiply_reduce_fusion.9
  92.3 0.7 multiply_reduce_fusion.9
  93.1 0.7 multiply_reduce_fusion.9
  93.9 0.7 multiply_reduce_fusion.9
  94.8 0.7 multiply_reduce_fusion.9
  95.6 0.7 multiply_reduce_fusion.9
  96.4 0.7 multiply_reduce_fusion.9
  97.2 0.8 copy.13
  98.2 13.7 %while.51 = (s32[]{:T(128)}, f32[128,1024]{1,0:T(8,128)S(1)}, f32[256,1024]{1,0:T(8,128)S(1)}, f32[128,1024]{1,0:T(8,128)S(1)}, s32[]{:T(128)}, /*index=5*/s32[]...) while((s32[]{:T(128)}, f32[128,1024]{1,0:T(8,128)S(1)}, ...), condition=%wide.region_1.2_spmd.clone, body=%wide.region_0.1_spmd.clone.sunk | while | flops 2228299 | bytes 5342311 | solution.py:26
  98.3 0.7 fusion.29
  99.2 0.7 fusion.29
  100.0 0.7 fusion.29
  100.9 0.7 fusion.29
  101.8 0.7 fusion.29
  102.6 0.7 fusion.29
  103.5 0.7 fusion.29
  104.3 0.7 fusion.29
  105.2 0.7 fusion.29
  106.0 0.7 fusion.29
  106.9 0.7 fusion.29
  107.8 0.7 fusion.29
  108.6 0.7 fusion.29
  109.5 0.7 fusion.29
  110.3 0.7 fusion.29
  111.2 0.7 fusion.29
  111.9 9.5 %convolution_convert_fusion.1 = bf16[128,8192]{1,0:T(8,128)(2,1)} fusion(bf16[1024,8192]{1,0:T(8,128)(2,1)} %param.16, f32[128,1024]{1,0:T(8,128)S(1)} %get-tuple-element.437, bf16[128,1024]{1,0:T(8,128)(2,1)S(1)} %copy-done), kind=kOutput, calls=%fused_computation.42 | convolution fusion | flops 2148925440 | bytes 19660800 | tf_op jit(solution)/shard_map/dot_general | solution.py:39
  121.4 9.7 %convolution_convert_fusion = bf16[1024,8192]{1,0:T(8,128)(2,1)} fusion(bf16[128,8192]{1,0:T(8,128)(2,1)} %all-gather.2.cloned.1.call-done, f32[128,1024]{1,0:T(8,128)S(1)} %get-tuple-element.437, bf16[128,1024]{1,0:T(8,128)(2,1)S(1)} %copy-done), kind=kOutput, calls=%fused_computation.41 | convolution fusion | flops 2156265472 | bytes 19660800 | tf_op jit(solution)/shard_map/dot_general | solution.py:73
  131.2 0.8 multiply_convert_fusion
  131.9 54.0 %all-reduce.2.cloned.1.call-done = bf16[1024,128]{1,0:T(8,128)(2,1)} async-done(((bf16[1024,128]{1,0:T(8,128)(2,1)}), bf16[1024,128]{1,0:T(8,128)(2,1)}) %all-reduce.2.cloned.1.call-update) | async-done | bytes 262160 | tf_op jit(solution)/shard_map/psum | solution.py:72
  186.0 1.8 convert_element_type.70
  187.7 32.5 %reduce-scatter.3.cloned.1.call-done = bf16[128,1024]{1,0:T(8,128)(2,1)} async-done(((bf16[128,8192]{1,0:T(8,128)(2,1)}), bf16[128,1024]{1,0:T(8,128)(2,1)}) %reduce-scatter.3.cloned.1.call-update) | async-done | bytes 262160 | tf_op jit(solution)/shard_map/reduce_scatter | solution.py:40
  220.3 116.5 %reduce-scatter.5.cloned.1.call-done = bf16[1024,512]{1,0:T(8,128)(2,1)} async-done(((bf16[1024,8192]{1,0:T(8,128)(2,1)}), bf16[1024,512]{1,0:T(8,128)(2,1)}) %reduce-scatter.5.cloned.1.call-update) | async-done | bytes 1048592 | tf_op jit(solution)/shard_map/reduce_scatter | solution.py:76
  (86 shorter events, 5.8 us)
Async XLA Ops:
  7.2 44.6 %copy-start.1 = (bf16[1024,128]{1,0:T(8,128)(2,1)S(1)}, bf16[1024,128]{1,0:T(8,128)(2,1)}, u32[]{:S(2)}) copy-start(bf16[1024,128]{1,0:T(8,128)(2,1)} %param.15) | copy-start | bytes 786436
  7.2 31.3 %all-gather.2.cloned.1.call-start = ((), (), s32[]{:S(2)}) async-start(), calls=%async_computation.3 | async-start | bytes 2359296 | tf_op jit(solution)/shard_map/all_gather | solution.py:43
  7.9 178.1 %all-reduce.2.cloned.1.call-start = ((), (), s32[]{:S(2)}) async-start(), calls=%async_computation.4 | async-start | bytes 524288 | tf_op jit(solution)/shard_map/psum | solution.py:72
  50.5 9.5 %collective-permute-start.1 = (bf16[128,1024]{1,0:T(8,128)(2,1)S(1)}, bf16[128,1024]{1,0:T(8,128)(2,1)S(1)}, u32[]{:S(2)}, u32[]{:S(2)}) collective-permute-start(bf16[128,1024]{1,0:T(8,128)(2,1)S(1)} %get-tuple-element.503), channel_id=1, source_target_pairs={{8,0},{16,8},{24,16},{32,24},{40,32},{48,40},{56,48},{64,56},{72,6... | collective-permute-start | bytes 786440 | tf_op jit(solution)/shard_map/ppermute | solution.py:10
  75.1 7.6 %collective-permute-start = (bf16[128,1024]{1,0:T(8,128)(2,1)S(1)}, bf16[128,1024]{1,0:T(8,128)(2,1)}, u32[]{:S(2)}, u32[]{:S(2)}) collective-permute-start(bf16[128,1024]{1,0:T(8,128)(2,1)S(1)} %get-tuple-element.522), channel_id=1, source_target_pairs={{0,8},{8,16},{16,24},{24,32},{32,40},{40,48},{48,56},{56,64},{64,7... | collective-permute-start | bytes 786440 | tf_op jit(solution)/shard_map/ppermute | solution.py:10
  97.2 14.6 %copy-start = (bf16[128,1024]{1,0:T(8,128)(2,1)S(1)}, bf16[128,1024]{1,0:T(8,128)(2,1)}, u32[]{:S(2)}) copy-start(bf16[128,1024]{1,0:T(8,128)(2,1)} %param.12) | copy-start | bytes 786436
  98.1 122.2 %reduce-scatter.3.cloned.1.call-start = ((), (), s32[]{:S(2)}) async-start(), calls=%async_computation.2 | async-start | bytes 2359296 | tf_op jit(solution)/shard_map/reduce_scatter | solution.py:40
  121.4 215.4 %reduce-scatter.5.cloned.1.call-start = ((), (), s32[]{:S(2)}) async-start(), calls=%async_computation.5 | async-start | bytes 17825792 | tf_op jit(solution)/shard_map/reduce_scatter | solution.py:76
Sparse Core Ops, SparseCore 0:
  9.7 28.7 all-gather.1
  98.2 87.6 all-reduce.1
  189.1 31.1 reduce-scatter.2
  224.5 112.2 reduce-scatter.4
where the time goes:
time: 344 us; the launch traced here: 343 us
  waiting for transfers between devices  246 us (72%)
  other arithmetic  38.3 us (11%)
  matrix products  31.2 us (9%)
  between operations  13.9 us (4%)
  starting transfers between devices  5.25 us (2%)
  loops' own time  4.91 us (1%)
  local copies, waits for them, and re-layouts  3.6 us (1%)
    reduce_scatter x1, waiting for transfers between devices, per_device(): lax.psum_scatter(partial_weight.astype(jnp.bfloat16), 'ctx', scatter_dime...  117 us
    psum x1, waiting for transfers between devices, per_device(): lax.psum(local_grad.astype(jnp.bfloat16), 'ctx').astype(jnp.float32)  54 us
    reduce_scatter x1, waiting for transfers between devices, per_device(): lax.psum_scatter(partial_value.astype(jnp.bfloat16), 'chan', scatter_dime...  32.5 us
    all_gather x1, waiting for transfers between devices, per_device(): full_cot = lax.all_gather(cotangent, 'chan', axis=1, tiled=True)  30.5 us
    add x32, other arithmetic, one_group(): running + rows * lax.dynamic_index_in_dim(taps_t, offset, 0, False)  21.5 us
    dot_general x1, matrix products, per_device(): lax.dot_general(full_cot, out_weight, (((1,), (1,)), ((), ())), preferred...  12 us
    ppermute x2, waiting for transfers between devices, passed_along(): return lax.ppermute(block, axis, route)  11.8 us
    reduce_sum x16, other arithmetic, tap_group(): rows.append(jnp.sum(grad_float * source, axis=0))  11 us
  transfers between devices with their start and end apart: 6, of which 6 were waited for; matrix products, arithmetic and copies ran while one was open for 10% of the time, Pallas kernels for 0%

commit v1 on v0

v1 whole, which is shorter than its diff:
```python
import functools

import jax
import jax.numpy as jnp
import numpy as np
from jax import lax
from jax.experimental import pallas as pl
from jax.experimental.pallas import tpu as pltpu
from jax.sharding import PartitionSpec as P

MESH = pl.DeviceIdType.MESH
BF = jnp.bfloat16
F32 = jnp.float32

TOK = 128
CH = 1024
TAPS = 128
N = 256
NCTX = 16
NCHAN = 8
COLS = 512
CC_W = 256
NC = CH // CC_W


def transforms():
    k = np.arange(128, dtype=np.float64)[:, None] + 0.5
    n = np.arange(N, dtype=np.float64)[None, :]
    angle = 2.0 * np.pi * k * n / N
    forward = np.concatenate([np.cos(angle), -np.sin(angle)], axis=0)
    inverse = forward.T / 128.0

    def split(m):
        high = m.astype(jnp.bfloat16)
        low = (m - high.astype(np.float64)).astype(jnp.bfloat16)
        return np.stack([high, low])

    return split(forward), split(inverse)


class Sems:
    def __init__(self):
        self.count = 0

    def take(self, n):
        base = self.count
        self.count += n
        return base


LAYOUT = Sems()
S_HALO = LAYOUT.take(NC)
S_COT = LAYOUT.take(3)
S_COTS = LAYOUT.take(4)
S_A2A = LAYOUT.take(16)
S_X3 = LAYOUT.take(3)
S_X3S = LAYOUT.take(4)
S_AG = LAYOUT.take(NC * 16)
S_MS = LAYOUT.take(4)
S_RS = LAYOUT.take(4)
S_GH = LAYOUT.take(NC)
S_LG = LAYOUT.take(16)
S_FG = LAYOUT.take(16)
N_SEMS = LAYOUT.count


def dot(a, b):
    return jnp.dot(a, b, preferred_element_type=F32)


def dot_nt(a, b):
    return lax.dot_general(a, b, (((1,), (1,)), ((), ())), preferred_element_type=F32)


def kernel(q_in, k_in, v_in, f_in, w_in, cot_in, ef_in, ei_in,
           mixed_o, gq_o, gk_o, gv_o, gf_o, gw_o,
           q, k, v, f, w, cot, ef, ei,
           pext, phat, fhat, ghat, filt, gated, gt, cc,
           part, mself, msib, rsend, rrecv, gg, gfb, gnext, lg, rg, fg, fgo,
           mixed_b, gq_b, gk_b, gv_b, gw_acc, gw_b,
           ld, wl, st, ss, rs):
    s = lax.axis_index("ctx")
    i = lax.axis_index("chan")
    z, y = s // 4, lax.rem(s, 4)
    x, c = i // 2, lax.rem(i, 2)
    sib = x * 2 + (1 - c)

    def ctx_at(dz, dy):
        return lax.rem(z + dz, 4) * 4 + lax.rem(y + dy, 4)

    def chan_at(dx):
        return lax.rem(x + dx, 4) * 2 + c

    barrier = pltpu.get_barrier_semaphore()

    def greet(d, carry):
        pl.semaphore_signal(barrier, inc=1, device_id=(lax.rem(s + d, NCTX), i), device_id_type=MESH)
        return carry

    for dx in (1, 2, 3):
        pl.semaphore_signal(barrier, inc=1, device_id=(s, chan_at(dx)), device_id_type=MESH)
    pl.semaphore_signal(barrier, inc=1, device_id=(s, sib), device_id_type=MESH)
    lax.fori_loop(1, NCTX, greet, 0)

    loads = {}

    def load(name, src, dst, slot):
        loads[name] = pltpu.make_async_copy(src, dst, ld.at[slot])
        loads[name].start()

    load("k", k_in, k, 0)
    load("v", v_in, v, 1)
    load("ef", ef_in, ef, 2)
    load("f", f_in, f, 3)
    load("ei", ei_in, ei, 4)
    load("q", q_in, q, 5)
    load("cot", cot_in, cot.at[i], 6)
    w_loads = []
    for d in range(4):
        columns = pl.ds(d * 2048, 2048)
        copy = pltpu.make_async_copy(w_in.at[:, columns], w.at[:, columns], wl.at[d])
        copy.start()
        w_loads.append(copy)

    def remote(src, dst, slot, ctx, chan):
        return pltpu.make_async_remote_copy(
            src_ref=src, dst_ref=dst, send_sem=ss.at[slot], recv_sem=rs.at[slot],
            device_id=(ctx, chan), device_id_type=MESH)

    sends = []

    def send(src, dst, slot, ctx, chan):
        copy = remote(src, dst, slot, ctx, chan)
        copy.start()
        sends.append(copy)

    def arrived(dst, slot):
        remote(dst, dst, slot, s, sib).wait_recv()

    loads["k"].wait()
    loads["v"].wait()
    pext[pl.ds(TOK, TOK), :] = (k[...].astype(F32) * v[...].astype(F32)).astype(BF)
    loads["ef"].wait()
    loads["f"].wait()
    for n in range(NC):
        taps = f[pl.ds(n * CC_W, CC_W), :]
        fhat[:, pl.ds(n * CC_W, CC_W)] = dot_nt(ef[0, :, 0:TOK], taps) + dot_nt(ef[1, :, 0:TOK], taps)
    loads["ei"].wait()
    loads["q"].wait()
    loads["cot"].wait()

    pl.semaphore_wait(barrier, NCTX - 1 + 4)

    after, before = lax.rem(s + 1, NCTX), lax.rem(s + NCTX - 1, NCTX)
    for n in range(NC):
        columns = pl.ds(n * CC_W, CC_W)
        send(pext.at[pl.ds(TOK, TOK), columns], pext.at[pl.ds(0, TOK), columns], S_HALO + n, after, i)
    for dx in (1, 3, 2):
        send(cot.at[i], cot.at[i], S_COT + dx - 1, s, chan_at(dx))
    send(cot.at[i], cot.at[i], S_COTS, s, sib)

    has_before = jnp.where(s > 0, 1.0, 0.0).astype(BF)
    has_after = jnp.where(s < NCTX - 1, 1.0, 0.0).astype(BF)

    def inverse(rows, spectrum):
        high = spectrum.astype(BF)
        low = (spectrum - high.astype(F32)).astype(BF)
        return dot(ei[0, rows, :], high) + (dot(ei[0, rows, :], low) + dot(ei[1, rows, :], high))

    lower, upper = slice(0, TOK), slice(TOK, N)

    def step_first(n, d):
        return ctx_at(0, d) if n < 2 else ctx_at(d, 0)

    def step_second(n, d):
        return ctx_at(d, 0) if n < 2 else ctx_at(0, d)

    def ag_slot(n, d, e):
        return S_AG + n * 16 + d * 4 + e

    for n in range(NC):
        columns = pl.ds(n * CC_W, CC_W)
        arrived(pext.at[pl.ds(0, TOK), columns], S_HALO + n)
        halo = pext[pl.ds(0, TOK), columns] * has_before
        both = jnp.concatenate([halo, pext[pl.ds(TOK, TOK), columns]], axis=0)
        spectrum = dot(ef[0], both) + dot(ef[1], both)
        phat[:, columns] = spectrum
        taps = fhat[:, columns]
        pr, pi, fr, fi = spectrum[:128], spectrum[128:], taps[:128], taps[128:]
        filtered = inverse(upper, jnp.concatenate([pr * fr - pi * fi, pr * fi + pi * fr], axis=0))
        filt[:, columns] = filtered
        value = q[:, columns].astype(F32) * filtered
        gated[:, columns] = value.astype(BF)
        gt[s, columns, :] = value.T.astype(BF)
        for d in (1, 3, 2):
            send(gt.at[s, columns, :], gt.at[s, columns, :], ag_slot(n, d, 0), step_first(n, d), i)
        for e in (1, 3, 2):
            send(gt.at[s, columns, :], gt.at[s, columns, :], ag_slot(n, 0, e), step_second(n, e), i)

    def forward_gated(n):
        columns = pl.ds(n * CC_W, CC_W)
        for d in (1, 3, 2):
            block = step_first(n, 4 - d)
            arrived(gt.at[block, columns, :], ag_slot(n, d, 0))
            for e in (1, 3, 2):
                send(gt.at[block, columns, :], gt.at[block, columns, :], ag_slot(n, d, e), step_second(n, e), i)

    def forward_cot(dx):
        block = chan_at(4 - dx)
        arrived(cot.at[block], S_COT + dx - 1)
        send(cot.at[block], cot.at[block], S_COTS + dx, s, sib)

    for copy in w_loads:
        copy.wait()

    def wide(d):
        return pl.ds(pl.multiple_of(d * CH, CH), CH)

    def mixed_part(dx):
        own = chan_at(dx)
        other = lax.rem(x + dx, 4) * 2 + (1 - c)
        part[dx] = dot(gated[...], w[:, wide(other)]).astype(BF)
        send(part.at[dx], msib.at[dx], S_MS + dx, s, sib)
        mself[...] = dot(gated[...], w[:, wide(own)])

    def mixed_send(dx):
        arrived(msib.at[dx], S_MS + dx)
        rsend[dx] = (mself[...] + msib[dx].astype(F32)).astype(BF)
        send(rsend.at[dx], rrecv.at[dx], S_RS + dx, s, chan_at(dx))

    mixed_part(2)
    forward_gated(0)
    mixed_send(2)
    mixed_part(1)
    forward_gated(2)
    mixed_send(1)
    forward_cot(1)
    forward_cot(3)
    mixed_part(3)
    forward_gated(1)
    mixed_send(3)
    forward_gated(3)
    mixed_part(0)
    arrived(msib.at[0], S_MS)
    mself[...] = mself[...] + msib[0].astype(F32)
    forward_cot(2)

    gg[...] = dot_nt(cot[i], w[:, wide(i)])
    for dx in (0, 1, 3, 2):
        if dx:
            own = chan_at(4 - dx)
            gg[...] += dot_nt(cot[own], w[:, wide(own)])
        other = lax.rem(x + 4 - dx, 4) * 2 + (1 - c)
        arrived(cot.at[other], S_COTS + dx)
        gg[...] += dot_nt(cot[other], w[:, wide(other)])

    mine = pl.ds(pl.multiple_of(i * 16, 16), 16)

    def columns_of(target):
        return cot.at[target // 2, mine, pl.ds(pl.multiple_of(lax.rem(target, 2) * COLS, COLS), COLS)]

    def spread(d, carry):
        target = lax.rem(s + d, NCTX)
        remote(columns_of(target), cc.at[s, mine, :], S_A2A + d, target, i).start()
        return carry

    lax.fori_loop(1, NCTX, spread, 0)
    keep = pltpu.make_async_copy(columns_of(s), cc.at[s, mine, :], ld.at[7])
    keep.start()

    grad = gg[...]
    gq_b[...] = (grad * filt[...]).astype(BF)
    gfb[...] = (grad * q[...].astype(F32)).astype(BF)
    outs = []

    def store(src, dst, slot):
        copy = pltpu.make_async_copy(src, dst, st.at[slot])
        copy.start()
        outs.append(copy)

    store(gq_b, gq_o, 0)
    for n in range(NC):
        columns = pl.ds(n * CC_W, CC_W)
        send(gfb.at[:, columns], gnext.at[:, columns], S_GH + n, before, i)
    for n in range(NC):
        columns = pl.ds(n * CC_W, CC_W)
        block = gfb[:, columns]
        g = dot(ef[0, :, 0:TOK], block) + dot(ef[1, :, 0:TOK], block)
        ghat[:, columns] = g
        p = phat[:, columns]
        pr, pi, gr, gi = p[:128], p[128:], g[:128], g[128:]
        taps = inverse(upper, jnp.concatenate([gr * pr + gi * pi, gi * pr - gr * pi], axis=0))
        lg[columns, :] = (-taps).T.astype(BF)

    def rows_of(target):
        return pl.ds(pl.multiple_of(target * 64, 64), 64)

    def scatter(d, carry):
        target = lax.rem(s + d, NCTX)
        remote(lg.at[rows_of(target), :], rg.at[s], S_LG + d, target, i).start()
        return carry

    lax.fori_loop(1, NCTX, scatter, 0)
    rg[s] = lg[rows_of(s), :]

    def spread_done(d, carry):
        source = lax.rem(s + NCTX - d, NCTX)
        remote(cc.at[source, mine, :], cc.at[source, mine, :], S_A2A + d, s, sib).wait_recv()
        return carry

    keep.wait()
    lax.fori_loop(1, NCTX, spread_done, 0)

    def share(chan):
        return cc.at[:, pl.ds(pl.multiple_of(chan * 16, 16), 16), :]

    for dx in (1, 3, 2):
        send(share(i), share(i), S_X3 + dx - 1, s, chan_at(dx))
    send(share(i), share(i), S_X3S, s, sib)

    def scatter_done(d, carry):
        source = lax.rem(s + NCTX - d, NCTX)
        remote(rg.at[source], rg.at[source], S_LG + d, s, sib).wait_recv()
        return carry

    lax.fori_loop(1, NCTX, scatter_done, 0)
    total = rg[0].astype(F32)
    for b in range(1, NCTX):
        total = total + rg[b].astype(F32)
    fg[rows_of(s), :] = total.astype(BF)

    def publish(d, carry):
        remote(fg.at[rows_of(s), :], fg.at[rows_of(s), :], S_FG + d, lax.rem(s + d, NCTX), i).start()
        return carry

    lax.fori_loop(1, NCTX, publish, 0)

    for n in range(NC):
        columns = pl.ds(n * CC_W, CC_W)
        arrived(gnext.at[:, columns], S_GH + n)
        block = gnext[:, columns] * has_after
        g = ghat[:, columns] + (dot(ef[0, :, TOK:N], block) + dot(ef[1, :, TOK:N], block))
        taps = fhat[:, columns]
        gr, gi, fr, fi = g[:128], g[128:], taps[:128], taps[128:]
        grad_product = inverse(lower, jnp.concatenate([gr * fr + gi * fi, gi * fr - gr * fi], axis=0))
        gk_b[:, columns] = (grad_product * v[:, columns].astype(F32)).astype(BF)
        gv_b[:, columns] = (grad_product * k[:, columns].astype(F32)).astype(BF)
    store(gk_b, gk_o, 1)
    store(gv_b, gv_o, 2)

    value = mself[...]
    for dx in (1, 3, 2):
        arrived(rrecv.at[dx], S_RS + dx)
        value = value + rrecv[dx].astype(F32)
    mixed_b[...] = value.astype(BF)
    store(mixed_b, mixed_o, 3)

    for dx in (1, 3, 2):
        block = chan_at(4 - dx)
        arrived(share(block), S_X3 + dx - 1)
        send(share(block), share(block), S_X3S + dx, s, sib)

    for n in range(NC):
        columns = pl.ds(n * CC_W, CC_W)
        for e in (1, 3, 2):
            for d in (0, 1, 3, 2):
                first, second = (4 - d) % 4, (4 - e) % 4
                block = ctx_at(second, first) if n < 2 else ctx_at(first, second)
                arrived(gt.at[block, columns, :], ag_slot(n, d, e))
    for dx in range(4):
        other = lax.rem(x + 4 - dx, 4) * 2 + (1 - c)
        arrived(share(other), S_X3S + dx)

    def weight_rows(n, carry):
        rows = pl.ds(pl.multiple_of(n * 256, 256), 256)
        left = jnp.concatenate([gt[b, rows, :] for b in range(NCTX)], axis=1)
        gw_b[rows, :] = dot(left, cc[...].reshape(NCTX * TOK, COLS)).astype(BF)
        return carry

    lax.fori_loop(0, 4, weight_rows, 0)
    store(gw_b, gw_o, 4)

    def publish_done(d, carry):
        rows = rows_of(lax.rem(s + NCTX - d, NCTX))
        remote(fg.at[rows, :], fg.at[rows, :], S_FG + d, s, sib).wait_recv()
        return carry

    lax.fori_loop(1, NCTX, publish_done, 0)
    fgo[...] = fg[...].astype(F32)
    store(fgo, gf_o, 5)

    for copy in sends:
        copy.wait_send()

    def sent(d, carry):
        remote(cc.at[0, mine, :], cc.at[0, mine, :], S_A2A + d, s, sib).wait_send()
        remote(rg.at[0], rg.at[0], S_LG + d, s, sib).wait_send()
        remote(fg.at[rows_of(s), :], fg.at[rows_of(s), :], S_FG + d, s, sib).wait_send()
        return carry

    lax.fori_loop(1, NCTX, sent, 0)
    for copy in outs:
        copy.wait()


def per_device(forward, inverse, query_proj, key_proj, value_proj, filters, out_weight, cotangent):
    sds = jax.ShapeDtypeStruct
    tile = (TOK, CH)
    V = pltpu.VMEM
    anywhere = pl.BlockSpec(memory_space=pl.ANY)
    scratch = [
        V(tile, BF), V(tile, BF), V(tile, BF), V((CH, TAPS), BF), V((CH, NCHAN * CH), BF),
        V((NCHAN,) + tile, BF), V((2, N, N), BF), V((2, N, N), BF),
        V((N, CH), BF), V((N, CH), F32), V((N, CH), F32), V((N, CH), F32), V(tile, F32), V(tile, BF),
        V((NCTX, CH, TOK), BF), V((NCTX, TOK, COLS), BF),
        V((4,) + tile, BF), V(tile, F32), V((4,) + tile, BF), V((4,) + tile, BF), V((4,) + tile, BF),
        V(tile, F32), V(tile, BF), V(tile, BF), V((CH, TAPS), BF), V((NCTX, 64, TAPS), BF),
        V((CH, TAPS), BF), V((CH, TAPS), F32),
        V(tile, BF), V(tile, BF), V(tile, BF), V(tile, BF), V((8, 128), F32), V((CH, COLS), BF),
        pltpu.SemaphoreType.DMA((8,)), pltpu.SemaphoreType.DMA((4,)), pltpu.SemaphoreType.DMA((6,)),
        pltpu.SemaphoreType.DMA((N_SEMS,)), pltpu.SemaphoreType.DMA((N_SEMS,)),
    ]
    return pl.pallas_call(
        kernel,
        out_shape=(
            sds(tile, BF), sds(tile, BF), sds(tile, BF), sds(tile, BF),
            sds((CH, TAPS), F32), sds((CH, COLS), BF),
        ),
        in_specs=[anywhere] * 8,
        out_specs=(anywhere,) * 6,
        scratch_shapes=scratch,
        compiler_params=pltpu.CompilerParams(
            collective_id=0, has_side_effects=True, vmem_limit_bytes=60 * 2**20),
        cost_estimate=pl.CostEstimate(
            flops=7_000_000_000, bytes_accessed=24_000_000, transcendentals=0),
    )(query_proj, key_proj, value_proj, filters, out_weight, cotangent, forward, inverse)


def solution(mesh):
    forward, inverse = transforms()
    placed = (
        P("ctx", "chan"), P("ctx", "chan"), P("ctx", "chan"),
        P("chan", None), P("chan", None), P("ctx", "chan"),
    )

    def body(*args):
        return per_device(jnp.asarray(forward), jnp.asarray(inverse), *args)

    return jax.shard_map(
        body,
        mesh=mesh,
        in_specs=placed,
        out_specs=(
            P("ctx", "chan"), P("ctx", "chan"), P("ctx", "chan"), P("ctx", "chan"),
            P("chan", None), P("chan", "ctx"),
        ),
        check_vma=False,
    )
```

time: 344 us -> 86.5 us (0.25)
  waiting for transfers between devices: 246 us -> 0 us
  Pallas kernels: 0 us -> 74.7 us
  other arithmetic: 38.3 us -> 0 us
  matrix products: 31.2 us -> 0 us
  between operations: 13.9 us -> 0.64 us
  local copies, waits for them, and re-layouts: 3.6 us -> 10.8 us
  starting transfers between devices: 5.25 us -> 0 us
  loops' own time: 4.91 us -> 0 us
    reduce_scatter x2 -> x0, waiting for transfers between devices: 149 us -> none  [the longest x1 117 us: per_device(): lax.psum_scatter(partial_weight.astype(jnp.bfloat16), 'ctx', scatter_dime...]
    pallas_call x0 -> x1, Pallas kernels: none -> 74.7 us  [per_device(): pl.pallas_call(kernel, out_shape=(sds(tile, BF), sds(tile, BF), sds(tile,...]
    psum x1 -> x0, waiting for transfers between devices: 54 us -> none  [per_device(): lax.psum(local_grad.astype(jnp.bfloat16), 'ctx').astype(jnp.float32)]
    dot_general x3 -> x0, matrix products: 31.2 us -> none  [the longest x1 12 us: per_device(): lax.dot_general(full_cot, out_weight, (((1,), (1,)), ((), ())), preferred...]
    all_gather x1 -> x0, waiting for transfers between devices: 30.5 us -> none  [per_device(): full_cot = lax.all_gather(cotangent, 'chan', axis=1, tiled=True)]
    add x32 -> x0, other arithmetic: 21.5 us -> none  [one_group(): running + rows * lax.dynamic_index_in_dim(taps_t, offset, 0, False)]
    ppermute x2 -> x0, waiting for transfers between devices: 11.8 us -> none  [passed_along(): return lax.ppermute(block, axis, route)]
    reduce_sum x16 -> x0, other arithmetic: 11 us -> none  [tap_group(): rows.append(jnp.sum(grad_float * source, axis=0))]
  transfers between devices with their start and end apart: 6 -> 0, of which waited for: 6 -> 0; matrix products, arithmetic and copies ran while one was open for 10% -> 0% of each run, Pallas kernels for 0% -> 0%
where the time goes in v1:
time: 86.5 us; the launch traced here: 86.2 us
  Pallas kernels  74.7 us (86%)
  local copies, waits for them, and re-layouts  10.8 us (12%)
    pallas_call x1, Pallas kernels, per_device(): pl.pallas_call(kernel, out_shape=(sds(tile, BF), sds(tile, BF), sds(tile,...  74.7 us
    unnamed x6, local copies, waits for them, and re-layouts  10.8 us

profile of v1, /device:TPU:1, one launch (start us, length us, event | category | flops | bytes accessed | tf_op | source)
XLA Modules:
  0.0 86.2 jit_solution(9293968988509877794)
XLA Ops:
  0.6 74.7 %shard_map.127 = (bf16[128,1024]{1,0:T(8,128)(2,1)}, bf16[128,1024]{1,0:T(8,128)(2,1)}, bf16[128,1024]{1,0:T(8,128)(2,1)}, bf16[128,1024]{1,0:T(8,128)(2,1)}, f3...) custom-call(bf16[128,1024]{1,0:T(8,128)(2,1)} %q_in.1, bf16[128,1024]{1,0:T(8,128)(2,1)} %k_in.1, bf16[128,1024]{1,0:T(8,128)(2,1)} %v_in.1, ...), custom_call_target="tpu_custom_call" | custom-call | flops 7000000000 | bytes 24000000 | tf_op jit(solution)/shard_map/pallas_call | solution.py:423
  75.4 1.7 %copy.20 = bf16[128,1024]{1,0:T(8,128)(2,1)} copy(bf16[128,1024]{1,0:T(8,128)(2,1)} %get-tuple-element.12) | data formatting | bytes 524288
  77.0 1.7 %copy.21 = bf16[128,1024]{1,0:T(8,128)(2,1)} copy(bf16[128,1024]{1,0:T(8,128)(2,1)} %get-tuple-element.13) | data formatting | bytes 524288
  78.7 1.7 %copy.22 = bf16[128,1024]{1,0:T(8,128)(2,1)} copy(bf16[128,1024]{1,0:T(8,128)(2,1)} %get-tuple-element.14) | data formatting | bytes 524288
  80.4 1.7 %copy.23 = bf16[128,1024]{1,0:T(8,128)(2,1)} copy(bf16[128,1024]{1,0:T(8,128)(2,1)} %get-tuple-element.15) | data formatting | bytes 524288
  82.0 1.9 %copy.24 = f32[1024,128]{1,0:T(8,128)} copy(f32[1024,128]{1,0:T(8,128)} %get-tuple-element.16) | data formatting | bytes 1048576
  83.9 2.3 %copy.25 = bf16[1024,512]{1,0:T(8,128)(2,1)} copy(bf16[1024,512]{1,0:T(8,128)(2,1)} %get-tuple-element.17) | data formatting | bytes 2097152

commit v2 on v1

--- a/solution.py
+++ b/solution.py
@@ -73,12 +73,11 @@
 
 
 def kernel(q_in, k_in, v_in, f_in, w_in, cot_in, ef_in, ei_in,
-           mixed_o, gq_o, gk_o, gv_o, gf_o, gw_o,
+           mixed_b, gq_b, gk_b, gv_b, fgo, gw_b,
            q, k, v, f, w, cot, ef, ei,
            pext, phat, fhat, ghat, filt, gated, gt, cc,
-           part, mself, msib, rsend, rrecv, gg, gfb, gnext, lg, rg, fg, fgo,
-           mixed_b, gq_b, gk_b, gv_b, gw_acc, gw_b,
-           ld, wl, st, ss, rs):
+           part, mself, msib, rsend, rrecv, gg, gfb, gnext, lg, rg, fg,
+           ld, wl, ss, rs):
     s = lax.axis_index("ctx")
     i = lax.axis_index("chan")
     z, y = s // 4, lax.rem(s, 4)
@@ -101,6 +100,15 @@
         pl.semaphore_signal(barrier, inc=1, device_id=(s, chan_at(dx)), device_id_type=MESH)
     pl.semaphore_signal(barrier, inc=1, device_id=(s, sib), device_id_type=MESH)
     lax.fori_loop(1, NCTX, greet, 0)
+
+    def greet_source(d, carry):
+        @pl.when(jnp.logical_or(d != s, s // 2 != i))
+        def _():
+            pl.semaphore_signal(barrier, inc=1, device_id=(d, s // 2), device_id_type=MESH)
+
+        return carry
+
+    lax.fori_loop(0, NCTX, greet_source, 0)
 
     loads = {}
 
@@ -149,12 +157,54 @@
     loads["q"].wait()
     loads["cot"].wait()
 
-    pl.semaphore_wait(barrier, NCTX - 1 + 4)
+    pl.semaphore_wait(barrier, NCTX - 1 + 4 + jnp.where(s // 2 == i, 15, 16))
 
     after, before = lax.rem(s + 1, NCTX), lax.rem(s + NCTX - 1, NCTX)
     for n in range(NC):
         columns = pl.ds(n * CC_W, CC_W)
         send(pext.at[pl.ds(TOK, TOK), columns], pext.at[pl.ds(0, TOK), columns], S_HALO + n, after, i)
+    mine = pl.ds(pl.multiple_of(i * 16, 16), 16)
+
+    def spread_copy(d):
+        target, chan = 2 * i + d // NCHAN, lax.rem(d, NCHAN)
+        rows = pl.ds(pl.multiple_of(chan * 16, 16), 16)
+        columns = pl.ds(pl.multiple_of((d // NCHAN) * COLS, COLS), COLS)
+        return target, chan, pltpu.make_async_remote_copy(
+            src_ref=cot.at[i, rows, columns], dst_ref=cc.at[s, rows, :],
+            send_sem=ss.at[S_A2A + d], recv_sem=rs.at[S_A2A + s],
+            device_id=(target, chan), device_id_type=MESH)
+
+    def spread(d, carry):
+        target, chan, copy = spread_copy(d)
+
+        @pl.when(jnp.logical_or(target != s, chan != i))
+        def _():
+            copy.start()
+
+        return carry
+
+    def spread_sent(d, carry):
+        target, chan, copy = spread_copy(d)
+
+        @pl.when(jnp.logical_or(target != s, chan != i))
+        def _():
+            copy.wait_send()
+
+        return carry
+
+    def spread_done(b, carry):
+        @pl.when(jnp.logical_or(b != s, s // 2 != i))
+        def _():
+            remote(cc.at[b, mine, :], cc.at[b, mine, :], S_A2A + b, s, sib).wait_recv()
+
+        return carry
+
+    lax.fori_loop(0, 16, spread, 0)
+
+    @pl.when(s // 2 == i)
+    def _():
+        cc[s, mine, :] = cot[i, mine, pl.ds(pl.multiple_of(lax.rem(s, 2) * COLS, COLS), COLS)]
+
     for dx in (1, 3, 2):
         send(cot.at[i], cot.at[i], S_COT + dx - 1, s, chan_at(dx))
     send(cot.at[i], cot.at[i], S_COTS, s, sib)
@@ -210,6 +260,15 @@
         arrived(cot.at[block], S_COT + dx - 1)
         send(cot.at[block], cot.at[block], S_COTS + dx, s, sib)
 
+    lax.fori_loop(0, NCTX, spread_done, 0)
+
+    def share(chan):
+        return cc.at[:, pl.ds(pl.multiple_of(chan * 16, 16), 16), :]
+
+    for dx in (1, 3, 2):
+        send(share(i), share(i), S_X3 + dx - 1, s, chan_at(dx))
+    send(share(i), share(i), S_X3S, s, sib)
+
     for copy in w_loads:
         copy.wait()
 
@@ -254,31 +313,9 @@
         arrived(cot.at[other], S_COTS + dx)
         gg[...] += dot_nt(cot[other], w[:, wide(other)])
 
-    mine = pl.ds(pl.multiple_of(i * 16, 16), 16)
-
-    def columns_of(target):
-        return cot.at[target // 2, mine, pl.ds(pl.multiple_of(lax.rem(target, 2) * COLS, COLS), COLS)]
-
-    def spread(d, carry):
-        target = lax.rem(s + d, NCTX)
-        remote(columns_of(target), cc.at[s, mine, :], S_A2A + d, target, i).start()
-        return carry
-
-    lax.fori_loop(1, NCTX, spread, 0)
-    keep = pltpu.make_async_copy(columns_of(s), cc.at[s, mine, :], ld.at[7])
-    keep.start()
-
     grad = gg[...]
     gq_b[...] = (grad * filt[...]).astype(BF)
     gfb[...] = (grad * q[...].astype(F32)).astype(BF)
-    outs = []
-
-    def store(src, dst, slot):
-        copy = pltpu.make_async_copy(src, dst, st.at[slot])
-        copy.start()
-        outs.append(copy)
-
-    store(gq_b, gq_o, 0)
     for n in range(NC):
         columns = pl.ds(n * CC_W, CC_W)
         send(gfb.at[:, columns], gnext.at[:, columns], S_GH + n, before, i)
@@ -302,21 +339,6 @@
 
     lax.fori_loop(1, NCTX, scatter, 0)
     rg[s] = lg[rows_of(s), :]
-
-    def spread_done(d, carry):
-        source = lax.rem(s + NCTX - d, NCTX)
-        remote(cc.at[source, mine, :], cc.at[source, mine, :], S_A2A + d, s, sib).wait_recv()
-        return carry
-
-    keep.wait()
-    lax.fori_loop(1, NCTX, spread_done, 0)
-
-    def share(chan):
-        return cc.at[:, pl.ds(pl.multiple_of(chan * 16, 16), 16), :]
-
-    for dx in (1, 3, 2):
-        send(share(i), share(i), S_X3 + dx - 1, s, chan_at(dx))
-    send(share(i), share(i), S_X3S, s, sib)
 
     def scatter_done(d, carry):
         source = lax.rem(s + NCTX - d, NCTX)
@@ -345,15 +367,12 @@
         grad_product = inverse(lower, jnp.concatenate([gr * fr + gi * fi, gi * fr - gr * fi], axis=0))
         gk_b[:, columns] = (grad_product * v[:, columns].astype(F32)).astype(BF)
         gv_b[:, columns] = (grad_product * k[:, columns].astype(F32)).astype(BF)
-    store(gk_b, gk_o, 1)
-    store(gv_b, gv_o, 2)
 
     value = mself[...]
     for dx in (1, 3, 2):
         arrived(rrecv.at[dx], S_RS + dx)
         value = value + rrecv[dx].astype(F32)
     mixed_b[...] = value.astype(BF)
-    store(mixed_b, mixed_o, 3)
 
     for dx in (1, 3, 2):
         block = chan_at(4 - dx)
@@ -378,7 +397,6 @@
         return carry
 
     lax.fori_loop(0, 4, weight_rows, 0)
-    store(gw_b, gw_o, 4)
 
     def publish_done(d, carry):
         rows = rows_of(lax.rem(s + NCTX - d, NCTX))
@@ -387,19 +405,25 @@
 
     lax.fori_loop(1, NCTX, publish_done, 0)
     fgo[...] = fg[...].astype(F32)
-    store(fgo, gf_o, 5)
 
     for copy in sends:
         copy.wait_send()
 
     def sent(d, carry):
-        remote(cc.at[0, mine, :], cc.at[0, mine, :], S_A2A + d, s, sib).wait_send()
         remote(rg.at[0], rg.at[0], S_LG + d, s, sib).wait_send()
         remote(fg.at[rows_of(s), :], fg.at[rows_of(s), :], S_FG + d, s, sib).wait_send()
         return carry
 
     lax.fori_loop(1, NCTX, sent, 0)
-    for copy in outs:
+    lax.fori_loop(0, 16, spread_sent, 0)
+
+
+def write_out(*refs):
+    sources, targets, done = refs[:6], refs[6:12], refs[12]
+    copies = [pltpu.make_async_copy(a, b, done.at[n]) for n, (a, b) in enumerate(zip(sources, targets))]
+    for copy in copies:
+        copy.start()
+    for copy in copies:
         copy.wait()
 
 
@@ -415,25 +439,31 @@
         V((NCTX, CH, TOK), BF), V((NCTX, TOK, COLS), BF),
         V((4,) + tile, BF), V(tile, F32), V((4,) + tile, BF), V((4,) + tile, BF), V((4,) + tile, BF),
         V(tile, F32), V(tile, BF), V(tile, BF), V((CH, TAPS), BF), V((NCTX, 64, TAPS), BF),
-        V((CH, TAPS), BF), V((CH, TAPS), F32),
-        V(tile, BF), V(tile, BF), V(tile, BF), V(tile, BF), V((8, 128), F32), V((CH, COLS), BF),
-        pltpu.SemaphoreType.DMA((8,)), pltpu.SemaphoreType.DMA((4,)), pltpu.SemaphoreType.DMA((6,)),
+        V((CH, TAPS), BF),
+        pltpu.SemaphoreType.DMA((8,)), pltpu.SemaphoreType.DMA((4,)),
         pltpu.SemaphoreType.DMA((N_SEMS,)), pltpu.SemaphoreType.DMA((N_SEMS,)),
     ]
-    return pl.pallas_call(
+    shapes = [(tile, BF)] * 4 + [((CH, TAPS), F32), ((CH, COLS), BF)]
+    inside = pl.BlockSpec(memory_space=pltpu.VMEM)
+    results = pl.pallas_call(
         kernel,
-        out_shape=(
-            sds(tile, BF), sds(tile, BF), sds(tile, BF), sds(tile, BF),
-            sds((CH, TAPS), F32), sds((CH, COLS), BF),
-        ),
+        out_shape=tuple(V(shape, dtype) for shape, dtype in shapes),
         in_specs=[anywhere] * 8,
-        out_specs=(anywhere,) * 6,
+        out_specs=(inside,) * 6,
         scratch_shapes=scratch,
         compiler_params=pltpu.CompilerParams(
-            collective_id=0, has_side_effects=True, vmem_limit_bytes=60 * 2**20),
+            collective_id=0, has_side_effects=True, vmem_limit_bytes=50 * 2**20),
         cost_estimate=pl.CostEstimate(
             flops=7_000_000_000, bytes_accessed=24_000_000, transcendentals=0),
     )(query_proj, key_proj, value_proj, filters, out_weight, cotangent, forward, inverse)
+    return pl.pallas_call(
+        write_out,
+        out_shape=tuple(sds(shape, dtype) for shape, dtype in shapes),
+        in_specs=[inside] * 6,
+        out_specs=(anywhere,) * 6,
+        scratch_shapes=[pltpu.SemaphoreType.DMA((6,))],
+        compiler_params=pltpu.CompilerParams(vmem_limit_bytes=4 * 2**20),
+    )(*results)
 
 
 def solution(mesh):

time: 86.5 us -> 70.9 us (0.82); the launches traced: 86.2 us -> 69.6 us
  Pallas kernels: 74.7 us -> 64.2 us
  local copies, waits for them, and re-layouts: 10.8 us -> 4.74 us
    pallas_call x1 -> x2, Pallas kernels: 74.7 us -> 64.2 us  [the longest x1 62.7 us: per_device(): pl.pallas_call(kernel, out_shape=tuple((V(shape, dtype) for shape, dtype...]
    unnamed x6 -> x10, local copies, waits for them, and re-layouts: 10.8 us -> 4.74 us
where the time goes in v2:
time: 70.9 us; the launch traced here: 69.6 us
  Pallas kernels  64.2 us (91%)
  local copies, waits for them, and re-layouts  4.74 us (7%)
    pallas_call x1, Pallas kernels, per_device(): pl.pallas_call(kernel, out_shape=tuple((V(shape, dtype) for shape, dtype...  62.7 us
    unnamed x10, local copies, waits for them, and re-layouts  4.74 us
    pallas_call x1, Pallas kernels, per_device(): pl.pallas_call(write_out, out_shape=tuple((sds(shape, dtype) for shape, d...  1.54 us

profile of v2, /device:TPU:1, one launch (start us, length us, event | category | flops | bytes accessed | tf_op | source)
XLA Modules:
  0.0 69.6 jit_solution(5955234179797166912)
XLA Ops:
  0.6 0.0 copy-start
  0.6 0.9 %copy-done = bf16[128,1024]{1,0:T(8,128)(2,1)S(1)} copy-done((bf16[128,1024]{1,0:T(8,128)(2,1)S(1)}, bf16[128,1024]{1,0:T(8,128)(2,1)}, u32[]{:S(2)}) %copy-start) | copy-done | bytes 262168
  1.6 0.0 copy-start.1
  1.6 0.9 %copy-done.1 = bf16[128,1024]{1,0:T(8,128)(2,1)S(1)} copy-done((bf16[128,1024]{1,0:T(8,128)(2,1)S(1)}, bf16[128,1024]{1,0:T(8,128)(2,1)}, u32[]{:S(2)}) %copy-start.1) | copy-done | bytes 262168
  2.5 0.0 copy-start.2
  2.5 0.9 %copy-done.2 = bf16[128,1024]{1,0:T(8,128)(2,1)S(1)} copy-done((bf16[128,1024]{1,0:T(8,128)(2,1)S(1)}, bf16[128,1024]{1,0:T(8,128)(2,1)}, u32[]{:S(2)}) %copy-start.2) | copy-done | bytes 262168
  3.5 0.0 copy-start.3
  3.5 0.9 %copy-done.3 = bf16[1024,128]{1,0:T(8,128)(2,1)S(1)} copy-done((bf16[1024,128]{1,0:T(8,128)(2,1)S(1)}, bf16[1024,128]{1,0:T(8,128)(2,1)}, u32[]{:S(2)}) %copy-start.3) | copy-done | bytes 262168
  4.4 0.0 copy-start.4
  4.4 0.9 %copy-done.4 = bf16[128,1024]{1,0:T(8,128)(2,1)S(1)} copy-done((bf16[128,1024]{1,0:T(8,128)(2,1)S(1)}, bf16[128,1024]{1,0:T(8,128)(2,1)}, u32[]{:S(2)}) %copy-start.4) | copy-done | bytes 262168
  5.4 62.7 %shard_map.127 = (bf16[128,1024]{1,0:T(8,128)(2,1)S(1)}, bf16[128,1024]{1,0:T(8,128)(2,1)S(1)}, bf16[128,1024]{1,0:T(8,128)(2,1)S(1)}, bf16[128,1024]{1,0:T(8,12...) custom-call(bf16[128,1024]{1,0:T(8,128)(2,1)S(1)} %copy-done, bf16[128,1024]{1,0:T(8,128)(2,1)S(1)} %copy-done.1, ...), custom_call_target="tpu_custom_call" | custom-call | flops 7000000000 | bytes 24000000 | tf_op jit(solution)/shard_map/pallas_call | solution.py:448
  68.1 1.5 %shard_map.128 = (bf16[128,1024]{1,0:T(8,128)(2,1)}, bf16[128,1024]{1,0:T(8,128)(2,1)}, bf16[128,1024]{1,0:T(8,128)(2,1)}, bf16[128,1024]{1,0:T(8,128)(2,1)}, f3...) custom-call(bf16[128,1024]{1,0:T(8,128)(2,1)S(1)} %get-tuple-element.12.refs_0_, ...), custom_call_target="tpu_custom_call" | custom-call | tf_op jit(solution)/shard_map/pallas_call | solution.py:459
Async XLA Ops:
  0.6 1.0 %copy-start = (bf16[128,1024]{1,0:T(8,128)(2,1)S(1)}, bf16[128,1024]{1,0:T(8,128)(2,1)}, u32[]{:S(2)}) copy-start(bf16[128,1024]{1,0:T(8,128)(2,1)} %q_in.1) | copy-start | bytes 786436
  1.6 0.9 %copy-start.1 = (bf16[128,1024]{1,0:T(8,128)(2,1)S(1)}, bf16[128,1024]{1,0:T(8,128)(2,1)}, u32[]{:S(2)}) copy-start(bf16[128,1024]{1,0:T(8,128)(2,1)} %k_in.1) | copy-start | bytes 786436
  2.5 0.9 %copy-start.2 = (bf16[128,1024]{1,0:T(8,128)(2,1)S(1)}, bf16[128,1024]{1,0:T(8,128)(2,1)}, u32[]{:S(2)}) copy-start(bf16[128,1024]{1,0:T(8,128)(2,1)} %v_in.1) | copy-start | bytes 786436
  3.5 0.9 %copy-start.3 = (bf16[1024,128]{1,0:T(8,128)(2,1)S(1)}, bf16[1024,128]{1,0:T(8,128)(2,1)}, u32[]{:S(2)}) copy-start(bf16[1024,128]{1,0:T(8,128)(2,1)} %f_in.1) | copy-start | bytes 786436
  4.4 0.9 %copy-start.4 = (bf16[128,1024]{1,0:T(8,128)(2,1)S(1)}, bf16[128,1024]{1,0:T(8,128)(2,1)}, u32[]{:S(2)}) copy-start(bf16[128,1024]{1,0:T(8,128)(2,1)} %cot_in.1) | copy-start | bytes 786436

commit v3 on v2

--- a/solution.py
+++ b/solution.py
@@ -21,6 +21,7 @@
 COLS = 512
 CC_W = 256
 NC = CH // CC_W
+ORDER = (0, 2, 1, 3)
 
 
 def transforms():
@@ -50,14 +51,14 @@
 
 LAYOUT = Sems()
 S_HALO = LAYOUT.take(NC)
-S_COT = LAYOUT.take(3)
+S_COT = LAYOUT.take(4)
 S_COTS = LAYOUT.take(4)
 S_A2A = LAYOUT.take(16)
-S_X3 = LAYOUT.take(3)
+S_X3 = LAYOUT.take(4)
 S_X3S = LAYOUT.take(4)
-S_AG = LAYOUT.take(NC * 16)
+S_AG = LAYOUT.take(NC * 20)
 S_MS = LAYOUT.take(4)
-S_RS = LAYOUT.take(4)
+S_RS = LAYOUT.take(6)
 S_GH = LAYOUT.take(NC)
 S_LG = LAYOUT.take(16)
 S_FG = LAYOUT.take(16)
@@ -96,7 +97,7 @@
         pl.semaphore_signal(barrier, inc=1, device_id=(lax.rem(s + d, NCTX), i), device_id_type=MESH)
         return carry
 
-    for dx in (1, 2, 3):
+    for dx in (1, 3):
         pl.semaphore_signal(barrier, inc=1, device_id=(s, chan_at(dx)), device_id_type=MESH)
     pl.semaphore_signal(barrier, inc=1, device_id=(s, sib), device_id_type=MESH)
     lax.fori_loop(1, NCTX, greet, 0)
@@ -157,10 +158,10 @@
     loads["q"].wait()
     loads["cot"].wait()
 
-    pl.semaphore_wait(barrier, NCTX - 1 + 4 + jnp.where(s // 2 == i, 15, 16))
+    pl.semaphore_wait(barrier, NCTX - 1 + 3 + jnp.where(s // 2 == i, 15, 16))
 
     after, before = lax.rem(s + 1, NCTX), lax.rem(s + NCTX - 1, NCTX)
-    for n in range(NC):
+    for n in ORDER:
         columns = pl.ds(n * CC_W, CC_W)
         send(pext.at[pl.ds(TOK, TOK), columns], pext.at[pl.ds(0, TOK), columns], S_HALO + n, after, i)
     mine = pl.ds(pl.multiple_of(i * 16, 16), 16)
@@ -205,8 +206,8 @@
     def _():
         cc[s, mine, :] = cot[i, mine, pl.ds(pl.multiple_of(lax.rem(s, 2) * COLS, COLS), COLS)]
 
-    for dx in (1, 3, 2):
-        send(cot.at[i], cot.at[i], S_COT + dx - 1, s, chan_at(dx))
+    for m, dx in enumerate((1, 3)):
+        send(cot.at[i], cot.at[i], S_COT + m, s, chan_at(dx))
     send(cot.at[i], cot.at[i], S_COTS, s, sib)
 
     has_before = jnp.where(s > 0, 1.0, 0.0).astype(BF)
@@ -219,16 +220,116 @@
 
     lower, upper = slice(0, TOK), slice(TOK, N)
 
-    def step_first(n, d):
-        return ctx_at(0, d) if n < 2 else ctx_at(d, 0)
-
-    def step_second(n, d):
-        return ctx_at(d, 0) if n < 2 else ctx_at(0, d)
-
-    def ag_slot(n, d, e):
-        return S_AG + n * 16 + d * 4 + e
-
-    for n in range(NC):
+    def at(n, da, db):
+        return ctx_at(db, da) if n < 2 else ctx_at(da, db)
+
+    def gated_send(n, da, db, half, slot, to_a, to_b):
+        rows = pl.ds(n * CC_W, CC_W) if half is None else pl.ds(n * CC_W + half * 128, 128)
+        block = gt.at[at(n, da, db), rows, :]
+        send(block, block, S_AG + n * 20 + slot, at(n, to_a, to_b), i)
+
+    def gated_wait(n, da, db, half, slot):
+        rows = pl.ds(n * CC_W, CC_W) if half is None else pl.ds(n * CC_W + half * 128, 128)
+        arrived(gt.at[at(n, da, db), rows, :], S_AG + n * 20 + slot)
+
+    def along_second(n, t, da):
+        gated_send(n, da, 0, None, 4 + 4 * t, 0, 1)
+        gated_send(n, da, 0, None, 5 + 4 * t, 0, 3)
+
+    def gather_own(n):
+        gated_send(n, 0, 0, None, 0, 1, 0)
+        gated_send(n, 0, 0, None, 1, 3, 0)
+        along_second(n, 0, 0)
+
+    def gather_near(n):
+        gated_wait(n, 3, 0, None, 0)
+        gated_send(n, 3, 0, 0, 2, 1, 0)
+        along_second(n, 1, 3)
+        gated_wait(n, 1, 0, None, 1)
+        gated_send(n, 1, 0, 1, 3, 3, 0)
+        along_second(n, 2, 1)
+
+    def gather_far(n):
+        gated_wait(n, 2, 0, 0, 2)
+        gated_wait(n, 2, 0, 1, 3)
+        along_second(n, 3, 2)
+
+    offset_of = (0, 3, 1, 2)
+
+    def gather_pass(n, t):
+        da = offset_of[t]
+        gated_wait(n, da, 3, None, 4 + 4 * t)
+        gated_send(n, da, 3, 0, 6 + 4 * t, 0, 1)
+        gated_wait(n, da, 1, None, 5 + 4 * t)
+        gated_send(n, da, 1, 1, 7 + 4 * t, 0, 3)
+
+    def gather_end(n, t):
+        da = offset_of[t]
+        gated_wait(n, da, 2, 0, 6 + 4 * t)
+        gated_wait(n, da, 2, 1, 7 + 4 * t)
+
+    def x_near(view, slot, sib_slot):
+        for m, (source, target) in enumerate(((3, 1), (1, 3))):
+            block = chan_at(source)
+            arrived(view(block), slot + m)
+            send(view(block, m), view(block, m), slot + 2 + m, s, chan_at(target))
+            send(view(block), view(block), sib_slot + 1 + m, s, sib)
+
+    def x_far(view, slot, sib_slot):
+        block = chan_at(2)
+        for m in range(2):
+            arrived(view(block, m), slot + 2 + m)
+        send(view(block), view(block), sib_slot + 3, s, sib)
+
+    def cot_view(block, half=None):
+        return cot.at[block] if half is None else cot.at[block, pl.ds(half * 64, 64), :]
+
+    def share(block, half=None):
+        rows = pl.ds(pl.multiple_of(block * 16, 16), 16)
+        return cc.at[:, rows, :] if half is None else cc.at[pl.ds(half * 8, 8), rows, :]
+
+    def mixed_part(dx):
+        chip = lax.rem(x + dx, 4)
+        both = dot(gated[...], w[:, pl.ds(pl.multiple_of(chip * 2 * CH, 2 * CH), 2 * CH)])
+        first, second = both[:, :CH], both[:, CH:]
+        part[dx] = jnp.where(c == 0, second, first).astype(BF)
+        send(part.at[dx], msib.at[dx], S_MS + dx, s, sib)
+        mself[dx] = jnp.where(c == 0, first, second)
+
+    top, bottom = pl.ds(0, 64), pl.ds(64, 64)
+
+    def chip_sum(dx, rows):
+        return mself[dx, rows, :] + msib[dx, rows, :].astype(F32)
+
+    def mixed_send(m, dx, value):
+        rsend[m] = value.astype(BF)
+        send(rsend.at[m], rrecv.at[m], S_RS + m, s, chan_at(dx))
+
+    def mixed_far():
+        arrived(msib.at[2], S_MS + 2)
+        mixed_send(0, 1, chip_sum(2, top))
+        mixed_send(1, 3, chip_sum(2, bottom))
+
+    def mixed_near():
+        arrived(msib.at[1], S_MS + 1)
+        mixed_send(2, 1, chip_sum(1, bottom))
+        arrived(msib.at[3], S_MS + 3)
+        mixed_send(3, 3, chip_sum(3, top))
+
+    def mixed_last():
+        arrived(rrecv.at[0], S_RS)
+        mixed_send(4, 1, chip_sum(1, top) + rrecv[0].astype(F32))
+        arrived(rrecv.at[1], S_RS + 1)
+        mixed_send(5, 3, chip_sum(3, bottom) + rrecv[1].astype(F32))
+
+    def mixed_end():
+        arrived(msib.at[0], S_MS)
+        for m in (2, 3, 4, 5):
+            arrived(rrecv.at[m], S_RS + m)
+        mixed_b[top, :] = (chip_sum(0, top) + rrecv[4].astype(F32) + rrecv[3].astype(F32)).astype(BF)
+        mixed_b[bottom, :] = (chip_sum(0, bottom) + rrecv[2].astype(F32) + rrecv[5].astype(F32)).astype(BF)
+
+    def gated_chunk(n):
         columns = pl.ds(n * CC_W, CC_W)
         arrived(pext.at[pl.ds(0, TOK), columns], S_HALO + n)
         halo = pext[pl.ds(0, TOK), columns] * has_before
@@ -242,84 +343,32 @@
         value = q[:, columns].astype(F32) * filtered
         gated[:, columns] = value.astype(BF)
         gt[s, columns, :] = value.T.astype(BF)
-        for d in (1, 3, 2):
-            send(gt.at[s, columns, :], gt.at[s, columns, :], ag_slot(n, d, 0), step_first(n, d), i)
-        for e in (1, 3, 2):
-            send(gt.at[s, columns, :], gt.at[s, columns, :], ag_slot(n, 0, e), step_second(n, e), i)
-
-    def forward_gated(n):
-        columns = pl.ds(n * CC_W, CC_W)
-        for d in (1, 3, 2):
-            block = step_first(n, 4 - d)
-            arrived(gt.at[block, columns, :], ag_slot(n, d, 0))
-            for e in (1, 3, 2):
-                send(gt.at[block, columns, :], gt.at[block, columns, :], ag_slot(n, d, e), step_second(n, e), i)
-
-    def forward_cot(dx):
-        block = chan_at(4 - dx)
-        arrived(cot.at[block], S_COT + dx - 1)
-        send(cot.at[block], cot.at[block], S_COTS + dx, s, sib)
-
-    lax.fori_loop(0, NCTX, spread_done, 0)
-
-    def share(chan):
-        return cc.at[:, pl.ds(pl.multiple_of(chan * 16, 16), 16), :]
-
-    for dx in (1, 3, 2):
-        send(share(i), share(i), S_X3 + dx - 1, s, chan_at(dx))
-    send(share(i), share(i), S_X3S, s, sib)
-
-    for copy in w_loads:
-        copy.wait()
-
-    def wide(d):
-        return pl.ds(pl.multiple_of(d * CH, CH), CH)
-
-    def mixed_part(dx):
-        own = chan_at(dx)
-        other = lax.rem(x + dx, 4) * 2 + (1 - c)
-        part[dx] = dot(gated[...], w[:, wide(other)]).astype(BF)
-        send(part.at[dx], msib.at[dx], S_MS + dx, s, sib)
-        mself[...] = dot(gated[...], w[:, wide(own)])
-
-    def mixed_send(dx):
-        arrived(msib.at[dx], S_MS + dx)
-        rsend[dx] = (mself[...] + msib[dx].astype(F32)).astype(BF)
-        send(rsend.at[dx], rrecv.at[dx], S_RS + dx, s, chan_at(dx))
-
-    mixed_part(2)
-    forward_gated(0)
-    mixed_send(2)
-    mixed_part(1)
-    forward_gated(2)
-    mixed_send(1)
-    forward_cot(1)
-    forward_cot(3)
-    mixed_part(3)
-    forward_gated(1)
-    mixed_send(3)
-    forward_gated(3)
-    mixed_part(0)
-    arrived(msib.at[0], S_MS)
-    mself[...] = mself[...] + msib[0].astype(F32)
-    forward_cot(2)
-
-    gg[...] = dot_nt(cot[i], w[:, wide(i)])
-    for dx in (0, 1, 3, 2):
-        if dx:
-            own = chan_at(4 - dx)
-            gg[...] += dot_nt(cot[own], w[:, wide(own)])
-        other = lax.rem(x + 4 - dx, 4) * 2 + (1 - c)
-        arrived(cot.at[other], S_COTS + dx)
-        gg[...] += dot_nt(cot[other], w[:, wide(other)])
-
-    grad = gg[...]
-    gq_b[...] = (grad * filt[...]).astype(BF)
-    gfb[...] = (grad * q[...].astype(F32)).astype(BF)
-    for n in range(NC):
-        columns = pl.ds(n * CC_W, CC_W)
-        send(gfb.at[:, columns], gnext.at[:, columns], S_GH + n, before, i)
-    for n in range(NC):
+
+    def share_out():
+        lax.fori_loop(0, NCTX, spread_done, 0)
+        for m, dx in enumerate((1, 3)):
+            send(share(i), share(i), S_X3 + m, s, chan_at(dx))
+        send(share(i), share(i), S_X3S, s, sib)
+
+    def grad_gated_part(dx, slot):
+        chip = lax.rem(x + dx, 4)
+        arrived(cot.at[chip * 2 + (1 - c)], S_COTS + slot)
+        row = jnp.concatenate([cot[chip * 2], cot[chip * 2 + 1]], axis=1)
+        term = dot_nt(row, w[:, pl.ds(pl.multiple_of(chip * 2 * CH, 2 * CH), 2 * CH)])
+        if slot == 0:
+            gg[...] = term
+        else:
+            gg[...] += term
+
+    def gradients():
+        grad = gg[...]
+        gfb[...] = (grad * q[...].astype(F32)).astype(BF)
+        for n in range(NC):
+            columns = pl.ds(n * CC_W, CC_W)
+            send(gfb.at[:, columns], gnext.at[:, columns], S_GH + n, before, i)
+        gq_b[...] = (grad * filt[...]).astype(BF)
+
+    def filter_terms(n):
         columns = pl.ds(n * CC_W, CC_W)
         block = gfb[:, columns]
         g = dot(ef[0, :, 0:TOK], block) + dot(ef[1, :, 0:TOK], block)
@@ -337,27 +386,37 @@
         remote(lg.at[rows_of(target), :], rg.at[s], S_LG + d, target, i).start()
         return carry
 
-    lax.fori_loop(1, NCTX, scatter, 0)
-    rg[s] = lg[rows_of(s), :]
-
     def scatter_done(d, carry):
         source = lax.rem(s + NCTX - d, NCTX)
         remote(rg.at[source], rg.at[source], S_LG + d, s, sib).wait_recv()
         return carry
 
-    lax.fori_loop(1, NCTX, scatter_done, 0)
-    total = rg[0].astype(F32)
-    for b in range(1, NCTX):
-        total = total + rg[b].astype(F32)
-    fg[rows_of(s), :] = total.astype(BF)
-
     def publish(d, carry):
         remote(fg.at[rows_of(s), :], fg.at[rows_of(s), :], S_FG + d, lax.rem(s + d, NCTX), i).start()
         return carry
 
-    lax.fori_loop(1, NCTX, publish, 0)
-
-    for n in range(NC):
+    def publish_done(d, carry):
+        rows = rows_of(lax.rem(s + NCTX - d, NCTX))
+        remote(fg.at[rows, :], fg.at[rows, :], S_FG + d, s, sib).wait_recv()
+        return carry
+
+    def filters_out():
+        lax.fori_loop(1, NCTX, scatter, 0)
+        rg[s] = lg[rows_of(s), :]
+
+    def filters_sum():
+        lax.fori_loop(1, NCTX, scatter_done, 0)
+        total = rg[0].astype(F32)
+        for b in range(1, NCTX):
+            total = total + rg[b].astype(F32)
+        fg[rows_of(s), :] = total.astype(BF)
+        lax.fori_loop(1, NCTX, publish, 0)
+
+    def filters_end():
+        lax.fori_loop(1, NCTX, publish_done, 0)
+        fgo[...] = fg[...].astype(F32)
+
+    def product_gradient(n):
         columns = pl.ds(n * CC_W, CC_W)
         arrived(gnext.at[:, columns], S_GH + n)
         block = gnext[:, columns] * has_after
@@ -368,43 +427,76 @@
         gk_b[:, columns] = (grad_product * v[:, columns].astype(F32)).astype(BF)
         gv_b[:, columns] = (grad_product * k[:, columns].astype(F32)).astype(BF)
 
-    value = mself[...]
-    for dx in (1, 3, 2):
-        arrived(rrecv.at[dx], S_RS + dx)
-        value = value + rrecv[dx].astype(F32)
-    mixed_b[...] = value.astype(BF)
-
-    for dx in (1, 3, 2):
-        block = chan_at(4 - dx)
-        arrived(share(block), S_X3 + dx - 1)
-        send(share(block), share(block), S_X3S + dx, s, sib)
-
-    for n in range(NC):
-        columns = pl.ds(n * CC_W, CC_W)
-        for e in (1, 3, 2):
-            for d in (0, 1, 3, 2):
-                first, second = (4 - d) % 4, (4 - e) % 4
-                block = ctx_at(second, first) if n < 2 else ctx_at(first, second)
-                arrived(gt.at[block, columns, :], ag_slot(n, d, e))
-    for dx in range(4):
-        other = lax.rem(x + 4 - dx, 4) * 2 + (1 - c)
-        arrived(share(other), S_X3S + dx)
-
-    def weight_rows(n, carry):
-        rows = pl.ds(pl.multiple_of(n * 256, 256), 256)
+    def share_end():
+        for slot, dx in enumerate((0, 3, 1, 2)):
+            arrived(share(lax.rem(x + dx, 4) * 2 + (1 - c)), S_X3S + slot)
+
+    def weight_rows(n):
+        for t in range(4):
+            gather_end(n, t)
+        rows = pl.ds(n * CC_W, CC_W)
         left = jnp.concatenate([gt[b, rows, :] for b in range(NCTX)], axis=1)
         gw_b[rows, :] = dot(left, cc[...].reshape(NCTX * TOK, COLS)).astype(BF)
-        return carry
-
-    lax.fori_loop(0, 4, weight_rows, 0)
-
-    def publish_done(d, carry):
-        rows = rows_of(lax.rem(s + NCTX - d, NCTX))
-        remote(fg.at[rows, :], fg.at[rows, :], S_FG + d, s, sib).wait_recv()
-        return carry
-
-    lax.fori_loop(1, NCTX, publish_done, 0)
-    fgo[...] = fg[...].astype(F32)
+
+    for copy in w_loads:
+        copy.wait()
+    grad_gated_part(0, 0)
+    for n in ORDER:
+        gated_chunk(n)
+        gather_own(n)
+    x_near(cot_view, S_COT, S_COTS)
+    gather_near(0)
+    grad_gated_part(3, 1)
+    gather_near(2)
+    gather_pass(0, 0)
+    grad_gated_part(1, 2)
+    x_far(cot_view, S_COT, S_COTS)
+    share_out()
+    gather_near(1)
+    gather_far(0)
+    gather_pass(2, 0)
+    grad_gated_part(2, 3)
+    gather_near(3)
+    gather_far(2)
+    gradients()
+    gather_pass(0, 1)
+    gather_pass(2, 1)
+    for n in range(NC):
+        filter_terms(n)
+    filters_out()
+    gather_pass(1, 0)
+    gather_far(1)
+    gather_pass(3, 0)
+    gather_far(3)
+    mixed_part(2)
+    gather_pass(0, 2)
+    gather_pass(2, 2)
+    mixed_far()
+    mixed_part(1)
+    x_near(share, S_X3, S_X3S)
+    gather_pass(0, 3)
+    gather_pass(2, 3)
+    mixed_part(3)
+    mixed_near()
+    filters_sum()
+    gather_pass(1, 1)
+    gather_pass(3, 1)
+    mixed_part(0)
+    mixed_last()
+    x_far(share, S_X3, S_X3S)
+    gather_pass(1, 2)
+    gather_pass(3, 2)
+    for n in range(NC):
+        product_gradient(n)
+    gather_pass(1, 3)
+    gather_pass(3, 3)
+    share_end()
+    weight_rows(0)
+    weight_rows(2)
+    mixed_end()
+    filters_end()
+    weight_rows(1)
+    weight_rows(3)
 
     for copy in sends:
         copy.wait_send()
@@ -431,13 +523,13 @@
     sds = jax.ShapeDtypeStruct
     tile = (TOK, CH)
     V = pltpu.VMEM
-    anywhere = pl.BlockSpec(memory_space=pl.ANY)
+    anywhere = pl.BlockSpec(memory_space=pltpu.HBM)
     scratch = [
         V(tile, BF), V(tile, BF), V(tile, BF), V((CH, TAPS), BF), V((CH, NCHAN * CH), BF),
         V((NCHAN,) + tile, BF), V((2, N, N), BF), V((2, N, N), BF),
         V((N, CH), BF), V((N, CH), F32), V((N, CH), F32), V((N, CH), F32), V(tile, F32), V(tile, BF),
         V((NCTX, CH, TOK), BF), V((NCTX, TOK, COLS), BF),
-        V((4,) + tile, BF), V(tile, F32), V((4,) + tile, BF), V((4,) + tile, BF), V((4,) + tile, BF),
+        V((4,) + tile, BF), V((4,) + tile, F32), V((4,) + tile, BF), V((6, 64, CH), BF), V((6, 64, CH), BF),
         V(tile, F32), V(tile, BF), V(tile, BF), V((CH, TAPS), BF), V((NCTX, 64, TAPS), BF),
         V((CH, TAPS), BF),
         pltpu.SemaphoreType.DMA((8,)), pltpu.SemaphoreType.DMA((4,)),
@@ -452,7 +544,7 @@
         out_specs=(inside,) * 6,
         scratch_shapes=scratch,
         compiler_params=pltpu.CompilerParams(
-            collective_id=0, has_side_effects=True, vmem_limit_bytes=50 * 2**20),
+            collective_id=0, has_side_effects=True, vmem_limit_bytes=61 * 2**20),
         cost_estimate=pl.CostEstimate(
             flops=7_000_000_000, bytes_accessed=24_000_000, transcendentals=0),
     )(query_proj, key_proj, value_proj, filters, out_weight, cotangent, forward, inverse)

time: 70.9 us -> 61.5 us (0.87); the launches traced: 69.6 us -> 61.4 us
  local copies, waits for them, and re-layouts: 4.74 us -> 0 us
  Pallas kernels: 64.2 us -> 60.6 us
    unnamed x10 -> x0, local copies, waits for them, and re-layouts: 4.74 us -> none
    pallas_call x1, Pallas kernels: 62.7 us -> 59 us  [per_device(): pl.pallas_call(kernel, out_shape=tuple((V(shape, dtype) for shape, dtype...]
where the time goes in v3:
time: 61.5 us; the launch traced here: 61.4 us
  Pallas kernels  60.6 us (99%)
  between operations  0.8 us (1%)
    pallas_call x1, Pallas kernels, per_device(): pl.pallas_call(kernel, out_shape=tuple((V(shape, dtype) for shape, dtype...  59 us
    pallas_call x1, Pallas kernels, per_device(): pl.pallas_call(write_out, out_shape=tuple((sds(shape, dtype) for shape, d...  1.54 us

profile of v3, /device:TPU:1, one launch (start us, length us, event | category | flops | bytes accessed | tf_op | source)
XLA Modules:
  0.0 61.4 jit_solution(17592155592348557924)
XLA Ops:
  0.6 59.0 %shard_map.127 = (bf16[128,1024]{1,0:T(8,128)(2,1)S(1)}, bf16[128,1024]{1,0:T(8,128)(2,1)S(1)}, bf16[128,1024]{1,0:T(8,128)(2,1)S(1)}, bf16[128,1024]{1,0:T(8,12...) custom-call(bf16[128,1024]{1,0:T(8,128)(2,1)} %q_in.1, bf16[128,1024]{1,0:T(8,128)(2,1)} %k_in.1, ...), custom_call_target="tpu_custom_call" | custom-call | flops 7000000000 | bytes 24000000 | tf_op jit(solution)/shard_map/pallas_call | solution.py:540
  59.6 1.5 %shard_map.128 = (bf16[128,1024]{1,0:T(8,128)(2,1)}, bf16[128,1024]{1,0:T(8,128)(2,1)}, bf16[128,1024]{1,0:T(8,128)(2,1)}, bf16[128,1024]{1,0:T(8,128)(2,1)}, f3...) custom-call(bf16[128,1024]{1,0:T(8,128)(2,1)S(1)} %get-tuple-element.12.refs_0_, ...), custom_call_target="tpu_custom_call" | custom-call | tf_op jit(solution)/shard_map/pallas_call | solution.py:551

commit v4 on v3

--- a/solution.py
+++ b/solution.py
@@ -21,6 +21,7 @@
 COLS = 512
 CC_W = 256
 NC = CH // CC_W
+SPANS = ((0, 256), (512, 256), (256, 256), (768, 256))
 ORDER = (0, 2, 1, 3)
 
 
@@ -149,20 +150,13 @@
     loads["k"].wait()
     loads["v"].wait()
     pext[pl.ds(TOK, TOK), :] = (k[...].astype(F32) * v[...].astype(F32)).astype(BF)
-    loads["ef"].wait()
-    loads["f"].wait()
-    for n in range(NC):
-        taps = f[pl.ds(n * CC_W, CC_W), :]
-        fhat[:, pl.ds(n * CC_W, CC_W)] = dot_nt(ef[0, :, 0:TOK], taps) + dot_nt(ef[1, :, 0:TOK], taps)
-    loads["ei"].wait()
-    loads["q"].wait()
     loads["cot"].wait()
 
     pl.semaphore_wait(barrier, NCTX - 1 + 3 + jnp.where(s // 2 == i, 15, 16))
 
     after, before = lax.rem(s + 1, NCTX), lax.rem(s + NCTX - 1, NCTX)
     for n in ORDER:
-        columns = pl.ds(n * CC_W, CC_W)
+        columns = pl.ds(*SPANS[n])
         send(pext.at[pl.ds(TOK, TOK), columns], pext.at[pl.ds(0, TOK), columns], S_HALO + n, after, i)
     mine = pl.ds(pl.multiple_of(i * 16, 16), 16)
 
@@ -210,6 +204,13 @@
         send(cot.at[i], cot.at[i], S_COT + m, s, chan_at(dx))
     send(cot.at[i], cot.at[i], S_COTS, s, sib)
 
+    loads["ef"].wait()
+    loads["f"].wait()
+    for n in range(NC):
+        taps = f[pl.ds(n * CC_W, CC_W), :]
+        fhat[:, pl.ds(n * CC_W, CC_W)] = dot_nt(ef[0, :, 0:TOK], taps) + dot_nt(ef[1, :, 0:TOK], taps)
+    loads["ei"].wait()
+    loads["q"].wait()
     has_before = jnp.where(s > 0, 1.0, 0.0).astype(BF)
     has_after = jnp.where(s < NCTX - 1, 1.0, 0.0).astype(BF)
 
@@ -224,12 +225,14 @@
         return ctx_at(db, da) if n < 2 else ctx_at(da, db)
 
     def gated_send(n, da, db, half, slot, to_a, to_b):
-        rows = pl.ds(n * CC_W, CC_W) if half is None else pl.ds(n * CC_W + half * 128, 128)
+        start, size = SPANS[n]
+        rows = pl.ds(start, size) if half is None else pl.ds(start + half * (size // 2), size // 2)
         block = gt.at[at(n, da, db), rows, :]
         send(block, block, S_AG + n * 20 + slot, at(n, to_a, to_b), i)
 
     def gated_wait(n, da, db, half, slot):
-        rows = pl.ds(n * CC_W, CC_W) if half is None else pl.ds(n * CC_W + half * 128, 128)
+        start, size = SPANS[n]
+        rows = pl.ds(start, size) if half is None else pl.ds(start + half * (size // 2), size // 2)
         arrived(gt.at[at(n, da, db), rows, :], S_AG + n * 20 + slot)
 
     def along_second(n, t, da):
@@ -330,7 +333,7 @@
         mixed_b[bottom, :] = (chip_sum(0, bottom) + rrecv[2].astype(F32) + rrecv[5].astype(F32)).astype(BF)
 
     def gated_chunk(n):
-        columns = pl.ds(n * CC_W, CC_W)
+        columns = pl.ds(*SPANS[n])
         arrived(pext.at[pl.ds(0, TOK), columns], S_HALO + n)
         halo = pext[pl.ds(0, TOK), columns] * has_before
         both = jnp.concatenate([halo, pext[pl.ds(TOK, TOK), columns]], axis=0)
@@ -434,69 +437,78 @@
     def weight_rows(n):
         for t in range(4):
             gather_end(n, t)
-        rows = pl.ds(n * CC_W, CC_W)
+        rows = pl.ds(*SPANS[n])
         left = jnp.concatenate([gt[b, rows, :] for b in range(NCTX)], axis=1)
         gw_b[rows, :] = dot(left, cc[...].reshape(NCTX * TOK, COLS)).astype(BF)
 
     for copy in w_loads:
         copy.wait()
     grad_gated_part(0, 0)
-    for n in ORDER:
-        gated_chunk(n)
-        gather_own(n)
+    gated_chunk(0)
+    gather_own(0)
+    gated_chunk(2)
+    gather_own(2)
+    gated_chunk(1)
+    gather_own(1)
+    gated_chunk(3)
+    gather_own(3)
     x_near(cot_view, S_COT, S_COTS)
+    share_out()
     gather_near(0)
+    gather_near(2)
     grad_gated_part(3, 1)
-    gather_near(2)
     gather_pass(0, 0)
+    gather_pass(2, 0)
+    gather_near(1)
+    gather_near(3)
+    x_far(cot_view, S_COT, S_COTS)
     grad_gated_part(1, 2)
-    x_far(cot_view, S_COT, S_COTS)
-    share_out()
-    gather_near(1)
+    gather_pass(1, 0)
+    gather_pass(3, 0)
     gather_far(0)
-    gather_pass(2, 0)
+    gather_far(2)
     grad_gated_part(2, 3)
-    gather_near(3)
-    gather_far(2)
+    x_near(share, S_X3, S_X3S)
     gradients()
     gather_pass(0, 1)
     gather_pass(2, 1)
-    for n in range(NC):
-        filter_terms(n)
+    gather_pass(1, 1)
+    gather_pass(3, 1)
+    filter_terms(0)
+    filter_terms(1)
+    filter_terms(2)
+    filter_terms(3)
     filters_out()
-    gather_pass(1, 0)
     gather_far(1)
-    gather_pass(3, 0)
     gather_far(3)
     mixed_part(2)
     gather_pass(0, 2)
     gather_pass(2, 2)
     mixed_far()
     mixed_part(1)
-    x_near(share, S_X3, S_X3S)
+    gather_pass(1, 2)
+    gather_pass(3, 2)
+    mixed_part(3)
+    mixed_near()
+    x_far(share, S_X3, S_X3S)
     gather_pass(0, 3)
     gather_pass(2, 3)
-    mixed_part(3)
-    mixed_near()
-    filters_sum()
-    gather_pass(1, 1)
-    gather_pass(3, 1)
     mixed_part(0)
     mixed_last()
-    x_far(share, S_X3, S_X3S)
-    gather_pass(1, 2)
-    gather_pass(3, 2)
-    for n in range(NC):
-        product_gradient(n)
     gather_pass(1, 3)
     gather_pass(3, 3)
+    filters_sum()
+    product_gradient(0)
+    product_gradient(1)
+    product_gradient(2)
+    product_gradient(3)
     share_end()
     weight_rows(0)
     weight_rows(2)
     mixed_end()
-    filters_end()
     weight_rows(1)
     weight_rows(3)
+    filters_end()
 
     for copy in sends:
         copy.wait_send()

time: 61.5 us -> 58.6 us (0.953)
  the two profiles are of different devices: /device:TPU:1 before, /device:TPU:26 now
where the time goes in v4:
time: 58.6 us; the launch traced here: 58.5 us
  Pallas kernels  57.7 us (98%)
  between operations  0.8 us (1%)
    pallas_call x1, Pallas kernels, per_device(): pl.pallas_call(kernel, out_shape=tuple((V(shape, dtype) for shape, dtype...  56.1 us
    pallas_call x1, Pallas kernels, per_device(): pl.pallas_call(write_out, out_shape=tuple((sds(shape, dtype) for shape, d...  1.54 us

profile of v4, /device:TPU:26, one launch (start us, length us, event | category | flops | bytes accessed | tf_op | source)
XLA Modules:
  0.0 58.5 jit_solution(16503685395023592182)
XLA Ops:
  0.6 56.1 %shard_map.127 = (bf16[128,1024]{1,0:T(8,128)(2,1)S(1)}, bf16[128,1024]{1,0:T(8,128)(2,1)S(1)}, bf16[128,1024]{1,0:T(8,128)(2,1)S(1)}, bf16[128,1024]{1,0:T(8,12...) custom-call(bf16[128,1024]{1,0:T(8,128)(2,1)} %q_in.1, bf16[128,1024]{1,0:T(8,128)(2,1)} %k_in.1, ...), custom_call_target="tpu_custom_call" | custom-call | flops 7000000000 | bytes 24000000 | tf_op jit(solution)/shard_map/pallas_call | solution.py:552
  56.8 1.5 %shard_map.128 = (bf16[128,1024]{1,0:T(8,128)(2,1)}, bf16[128,1024]{1,0:T(8,128)(2,1)}, bf16[128,1024]{1,0:T(8,128)(2,1)}, bf16[128,1024]{1,0:T(8,128)(2,1)}, f3...) custom-call(bf16[128,1024]{1,0:T(8,128)(2,1)S(1)} %get-tuple-element.12.refs_0_, ...), custom_call_target="tpu_custom_call" | custom-call | tf_op jit(solution)/shard_map/pallas_call | solution.py:563

commit v5 on v4

--- a/solution.py
+++ b/solution.py
@@ -469,6 +469,8 @@
     gather_far(2)
     grad_gated_part(2, 3)
     x_near(share, S_X3, S_X3S)
+    gather_far(1)
+    gather_far(3)
     gradients()
     gather_pass(0, 1)
     gather_pass(2, 1)
@@ -479,8 +481,6 @@
     filter_terms(2)
     filter_terms(3)
     filters_out()
-    gather_far(1)
-    gather_far(3)
     mixed_part(2)
     gather_pass(0, 2)
     gather_pass(2, 2)

time: 58.6 us -> 62.8 us (1.072)
  the two profiles are of different devices: /device:TPU:26 before, /device:TPU:0 now
where the time goes in v5:
time: 62.8 us; the launch traced here: 62.7 us
  Pallas kernels  61.9 us (99%)
  between operations  0.8 us (1%)
    pallas_call x1, Pallas kernels, per_device(): pl.pallas_call(kernel, out_shape=tuple((V(shape, dtype) for shape, dtype...  60.4 us
    pallas_call x1, Pallas kernels, per_device(): pl.pallas_call(write_out, out_shape=tuple((sds(shape, dtype) for shape, d...  1.54 us

profile of v5, /device:TPU:0, one launch (start us, length us, event | category | flops | bytes accessed | tf_op | source)
XLA Modules:
  0.0 62.7 jit_solution(3136209120454514583)
XLA Ops:
  0.6 60.4 %shard_map.127 = (bf16[128,1024]{1,0:T(8,128)(2,1)S(1)}, bf16[128,1024]{1,0:T(8,128)(2,1)S(1)}, bf16[128,1024]{1,0:T(8,128)(2,1)S(1)}, bf16[128,1024]{1,0:T(8,12...) custom-call(bf16[128,1024]{1,0:T(8,128)(2,1)} %q_in.1, bf16[128,1024]{1,0:T(8,128)(2,1)} %k_in.1, ...), custom_call_target="tpu_custom_call" | custom-call | flops 7000000000 | bytes 24000000 | tf_op jit(solution)/shard_map/pallas_call | solution.py:552
  61.0 1.5 %shard_map.128 = (bf16[128,1024]{1,0:T(8,128)(2,1)}, bf16[128,1024]{1,0:T(8,128)(2,1)}, bf16[128,1024]{1,0:T(8,128)(2,1)}, bf16[128,1024]{1,0:T(8,128)(2,1)}, f3...) custom-call(bf16[128,1024]{1,0:T(8,128)(2,1)S(1)} %get-tuple-element.12.refs_0_, ...), custom_call_target="tpu_custom_call" | custom-call | tf_op jit(solution)/shard_map/pallas_call | solution.py:563
